TPU v7x, 32 devices: a whole 2x2x4 slice. The times are simulated.
32 devices in a mesh: row: 4 (over y, x), col: 8 (over z, core).
Axes of the slice: x: 2, y: 2, z: 4, core: 2. Of those that a mesh axis runs over, the one named last changes fastest.
Arguments:
- child_rhs: bfloat16 [1536, 128, 128], P(('row', 'col')), may hold values from -6 to 6
- parent_rhs: bfloat16 [8, 128, 128], P('col'), may hold values from -6 to 6
- child_lower_inv: bfloat16 [1536, 128, 128], P(('row', 'col')), may hold values from -0.5 to 0.5
- child_lower_off: bfloat16 [1536, 128, 128], P(('row', 'col')), may hold values from -0.125 to 0.125
- child_upper_inv: bfloat16 [1536, 128, 128], P(('row', 'col')), may hold values from -0.5 to 0.5
- child_upper_off: bfloat16 [1536, 128, 128], P(('row', 'col')), may hold values from -0.25 to 0.25
- parent_lower_inv: bfloat16 [8, 128, 128], P('col'), may hold values from -0.5 to 0.5
- parent_upper_inv: bfloat16 [8, 128, 128], P('col'), may hold values from -0.5 to 0.5
- parent_of: int32 [1536], P(('row', 'col')), may hold values from 0 to 7
Outputs:
- child_solution: bfloat16 [1536, 128, 128], P(('row', 'col'))
- parent_solution: bfloat16 [8, 128, 128], P('col')
Inputs may be any that keep to these rules, and one draw needn't show every extreme that they name: `parent_of`: each lower-level supernode names one upper-level parent.
All inputs are finite; a program needn't handle non-finite values.
Results may differ from a plain program's by a relative error of at most 0.0095.
Values may be sent and summed in bfloat16 or wider, within the bound.
No kernel may reach another device: no remote copies, remote signals or barrier semaphores. Data moves between devices by JAX's collectives and lax.ppermute only.
A program may use at most 64 MiB of HBM per device.

v0:
```python
import functools
import math
import jax
import jax.numpy as jnp
from jax import lax
from jax.experimental import pallas as pl
from jax.experimental.pallas import tpu as pltpu
from jax.sharding import Mesh, PartitionSpec as P

F32 = jnp.float32
BF16 = jnp.bfloat16
VMEM = pl.BlockSpec(memory_space=pltpu.VMEM)
ANY = pl.BlockSpec(memory_space=pl.ANY)
MIB = 1 << 20
VMEM_BYTES = 64 * MIB
WAIT = pl.CostEstimate(flops=8 * 10**9, bytes_accessed=MIB, transcendentals=0)


def ranges(count, shares):
    ends = [count * sum(shares[: i + 1]) // sum(shares) for i in range(len(shares))]
    pairs = zip([0] + ends[:-1], ends)
    return [(lo, hi) for lo, hi in pairs if hi > lo]


def params(mib):
    return pltpu.CompilerParams(vmem_limit_bytes=mib * MIB)


def dot(a, b):
    return jnp.dot(a, b, preferred_element_type=F32)


def dot_t(a, b):
    return lax.dot_general(a, b, (((1,), (1,)), ((), ())), preferred_element_type=F32)


def forward_kernel(cores, chunk, owner_hbm, rhs_hbm, inv_hbm, off_hbm, fwd, *rest):
    mine, theirs, scratch = rest[0], rest[1:cores], rest[cores:]
    rhs, inv, off, owner, even, odd, in_sem, owner_sem = scratch
    n_row, _, half, _ = mine.shape
    groups = fwd.shape[0] // chunk
    arrays = ((rhs_hbm, rhs), (inv_hbm, inv), (off_hbm, off))

    def load(s, g):
        part = pl.ds(g * chunk, chunk)
        return pltpu.make_async_copy(arrays[s][0].at[part], arrays[s][1].at[part], in_sem.at[s, g])

    load(0, 0).start()
    load(1, 0).start()
    names = pltpu.make_async_copy(owner_hbm, owner, owner_sem)
    names.start()

    @pl.loop(1, groups)
    def _(g):
        load(0, g).start()
        load(1, g).start()
        load(2, g - 1).start()

    load(2, groups - 1).start()
    even[...] = jnp.zeros_like(even)
    odd[...] = jnp.zeros_like(odd)

    def solve(c):
        fwd[c] = dot(inv[c], rhs[c]).astype(BF16)

    def add(c, acc):
        acc[owner[c]] += dot(off[c], fwd[c])

    load(0, 0).wait()
    load(1, 0).wait()
    for n in range(chunk):
        solve(n)
    names.wait()

    def step(g):
        load(0, g).wait()
        load(1, g).wait()
        load(2, g - 1).wait()
        for n in range(chunk):
            solve(g * chunk + n)
            add((g - 1) * chunk + n, odd if n % 2 else even)

    pl.loop(1, groups - 1)(step)
    if groups > 1:
        step(groups - 1)
    load(2, groups - 1).wait()
    for n in range(chunk):
        add((groups - 1) * chunk + n, odd if n % 2 else even)
    me = lax.axis_index("core")
    for p in range(even.shape[0]):
        turned = (even[p] + odd[p]).astype(BF16).T
        for r in range(n_row):
            halves = [turned[n * half : (n + 1) * half] for n in range(r * cores, (r + 1) * cores)]
            for k in range(cores):
                out = theirs[k - 1] if k else mine
                value = halves[0]
                for n in range(1, cores):
                    value = jnp.where(lax.rem(me + k, cores) == n, halves[n], value)
                out[r, p] = value


def forward(parent_of, rhs, inv, off, n_row, n_chip, cores, per_col):
    count, width, sides = rhs.shape
    chunk = max(c for c in range(1, 13) if count % c == 0)
    parents = n_chip * cores * per_col
    piece = (n_row, parents, sides // (n_row * cores), width)
    kept = 2 * rhs.size + 2 * cores * math.prod(piece)
    room = (VMEM_BYTES - kept - MIB) // MIB
    return pl.pallas_call(
        functools.partial(forward_kernel, cores, chunk),
        out_shape=[pltpu.VMEM(rhs.shape, BF16)] + [pltpu.VMEM(piece, BF16)] * cores,
        in_specs=[ANY] * 4,
        out_specs=[VMEM] * (1 + cores),
        scratch_shapes=[
            pltpu.VMEM(rhs.shape, BF16),
            pltpu.VMEM(inv.shape, BF16),
            pltpu.VMEM(off.shape, BF16),
            pltpu.SMEM(parent_of.shape, jnp.int32),
            pltpu.VMEM((parents, width, sides), F32),
            pltpu.VMEM((parents, width, sides), F32),
            pltpu.SemaphoreType.DMA((3, count // chunk)),
            pltpu.SemaphoreType.DMA,
        ],
        compiler_params=params(room),
        name="forward",
    )(*(pltpu.with_memory_space_constraint(x, pltpu.HBM) for x in (parent_of, rhs, inv, off)))


def couple_kernel(inv, off, _, out):
    for c in range(out.shape[0]):
        out[c] = (-dot(inv[c], off[c])).astype(BF16)


def couple(inv, off, after):
    count, width, _ = inv.shape
    return pl.pallas_call(
        couple_kernel,
        out_shape=pltpu.VMEM(off.shape, BF16),
        in_specs=[VMEM, VMEM, ANY],
        out_specs=VMEM,
        compiler_params=params(16),
        cost_estimate=pl.CostEstimate(
            flops=2 * count * width**3, bytes_accessed=6 * count * width**2, transcendentals=0
        ),
        name="couple",
    )(inv, off, after)


def core_sum_kernel(*refs):
    total = refs[0][...].astype(F32)
    for part in refs[1:-2]:
        total = total + part[...].astype(F32)
    refs[-1][...] = total.astype(BF16)


def core_sum(parts, after):
    return pl.pallas_call(
        core_sum_kernel,
        out_shape=jax.ShapeDtypeStruct(parts[0].shape, BF16),
        in_specs=[VMEM] * len(parts) + [ANY],
        out_specs=VMEM,
        compiler_params=params(16),
        cost_estimate=WAIT,
        name="core_sum",
    )(*parts, after)


def prepare_kernel(rhs, lower, upper, _, whole, mine, turned):
    slab = mine.shape[1]
    rows = pl.ds(pl.multiple_of(lax.axis_index("row") * slab, slab), slab)
    for p in range(mine.shape[0]):
        whole[p] = dot(upper[p], lower[p]).astype(BF16)
        turned[...] = rhs[p].astype(F32).T
        mine[p] = turned[rows, :]


def prepare(rhs, lower, upper, after, n_row):
    per_col, width, sides = rhs.shape
    return pl.pallas_call(
        prepare_kernel,
        out_shape=[
            jax.ShapeDtypeStruct(lower.shape, BF16),
            jax.ShapeDtypeStruct((per_col, sides // n_row, width), F32),
        ],
        in_specs=[VMEM] * 3 + [ANY],
        out_specs=[VMEM, VMEM],
        scratch_shapes=[pltpu.VMEM((sides, width), F32)],
        compiler_params=params(16),
        name="prepare",
    )(rhs, lower, upper, after)


def parent_kernel(cores, whole, rhs, parts, out):
    devices, per_col, half, _ = out.shape
    for p in range(per_col):
        updates = []
        for k in range(cores):
            terms = [parts[d, p].astype(F32) for d in range(k, devices, cores)]
            while len(terms) > 1:
                pairs = zip(terms[::2], terms[1::2])
                terms = [x + y for x, y in pairs] + terms[len(terms) - len(terms) % 2 :]
            updates.append(terms[0])
        residual = (rhs[p] - jnp.concatenate(updates)).astype(BF16)
        solved = dot_t(residual, whole[p]).astype(BF16)
        for d in range(devices):
            k = d % cores
            out[d, p] = solved[k * half : (k + 1) * half]


def parent_solve(whole, rhs, parts, cores):
    return pl.pallas_call(
        functools.partial(parent_kernel, cores),
        out_shape=jax.ShapeDtypeStruct(parts.shape, BF16),
        in_specs=[VMEM] * 3,
        out_specs=VMEM,
        compiler_params=params(16),
        cost_estimate=WAIT,
        name="parent_solve",
    )(whole, rhs, parts)


def backward_kernel(cores, groups, owner, fwd, inv, coupled, *rest):
    parts, scratch = rest[:cores], rest[cores:]
    out_hbm, solved_hbm, out, picked, out_sem, solved_sem = scratch
    n_row, parents, half, _ = parts[0].shape
    per_col = solved_hbm.shape[0]
    me = lax.axis_index("core")
    for p in range(parents):
        rows = []
        for r in range(n_row):
            for n in range(cores):
                value = parts[0][r, p]
                for k in range(1, cores):
                    value = jnp.where(lax.rem(me + k, cores) == n, parts[k][r, p], value)
                rows.append(value)
        picked[p] = jnp.concatenate(rows).T
    mine = (lax.axis_index("z") * cores + me) * per_col
    solved = pltpu.make_async_copy(picked.at[pl.ds(mine, per_col)], solved_hbm, solved_sem)
    solved.start()
    stores = [solved]
    for g, (lo, hi) in enumerate(groups):
        for c in range(lo, hi):
            mats = jnp.concatenate([inv[c], coupled[c]], axis=1)
            out[c] = dot(mats, jnp.concatenate([fwd[c], picked[owner[c]]])).astype(BF16)
        part = pl.ds(lo, hi - lo)
        copy = pltpu.make_async_copy(out.at[part], out_hbm.at[part], out_sem.at[g])
        copy.start()
        stores.append(copy)
    for copy in stores:
        copy.wait()


def backward(parent_of, fwd, inv, coupled, parts, per_col):
    count, width, sides = fwd.shape
    groups = ranges(count, (1, 2, 3, 4, 5, 4, 3, 2))
    parents = parts[0].shape[1]
    return pl.pallas_call(
        functools.partial(backward_kernel, len(parts), groups),
        out_shape=[
            jax.ShapeDtypeStruct(fwd.shape, BF16),
            jax.ShapeDtypeStruct((per_col, width, sides), BF16),
        ],
        in_specs=[VMEM] * (4 + len(parts)),
        out_specs=[ANY, ANY],
        scratch_shapes=[
            pltpu.VMEM(fwd.shape, BF16),
            pltpu.VMEM((parents, width, sides), BF16),
            pltpu.SemaphoreType.DMA((len(groups),)),
            pltpu.SemaphoreType.DMA,
        ],
        compiler_params=params(32),
        name="backward",
    )(parent_of, fwd, inv, coupled, *parts)


def from_core(value, k):
    cores = lax.axis_size("core")
    return lax.ppermute(value, "core", [(i, (i + k) % cores) for i in range(cores)])


def on_device(
    child_rhs,
    parent_rhs,
    child_lower_inv,
    child_lower_off,
    child_upper_inv,
    child_upper_off,
    parent_lower_inv,
    parent_upper_inv,
    parent_of,
):
    n_row, n_chip, cores = (lax.axis_size(a) for a in ("row", "z", "core"))
    per_col = parent_rhs.shape[0]
    fwd, mine, *theirs = forward(
        parent_of, child_rhs, child_lower_inv, child_lower_off, n_row, n_chip, cores, per_col
    )
    theirs = [from_core(x, k) for k, x in enumerate(theirs, 1)]
    whole, rhs = prepare(parent_rhs, parent_lower_inv, parent_upper_inv, mine, n_row)
    total = core_sum([mine] + theirs, whole)
    axes = ("row", "z", "core")
    sent = total.reshape(-1, per_col, *total.shape[2:])
    parts = lax.all_to_all(sent, axes, 0, 0, tiled=True)
    solved = parent_solve(whole, rhs, parts, cores)
    mine = lax.all_to_all(solved, axes, 0, 0, tiled=True).reshape(total.shape)
    parts = [mine] + [from_core(mine, cores - k) for k in range(1, cores)]
    coupled = couple(child_upper_inv, child_upper_off, mine)
    return tuple(backward(parent_of, fwd, child_upper_inv, coupled, parts, per_col))


def solution(mesh):
    n_row, n_col = (mesh.shape[a] for a in ("row", "col"))
    cores = 1 if n_col % 2 else 2
    split = Mesh(mesh.devices.reshape(n_row, n_col // cores, cores), ("row", "z", "core"))
    child = P(("row", "z", "core"), None, None)
    parent = P(("z", "core"), None, None)
    return jax.shard_map(
        on_device,
        mesh=split,
        in_specs=(child, parent, child, child, child, child, parent, parent, P(("row", "z", "core"))),
        out_specs=(child, parent),
        check_vma=False,
    )
```

profile of v0, /device:TPU:0, one launch (start us, length us, event | category | flops | bytes accessed | tf_op | source)
XLA Modules:
  0.0 33.9 jit_solution(16111493478561025699)
XLA Ops:
  0.6 0.0 copy-start.4
  0.6 0.0 copy-start.3
  0.7 0.0 copy-start.2
  0.7 3.1 %forward.1 = (bf16[48,128,128]{2,1,0:T(8,128)(2,1)S(1)}, bf16[4,8,16,128]{3,2,1,0:T(8,128)(2,1)S(1)}, bf16[4,8,16,128]{3,2,1,0:T(8,128)(2,1)S(1)}) custom-call(s32[48]{0:T(128)} %owner.1, bf16[48,128,128]{2,1,0:T(8,128)(2,1)} %rhs_hbm.1, bf16[48,128,128]{2,1,0:T(8,128)(2,1)} %inv_hbm.1, bf16[48,128,128]{2,1,0:T(8,128)(2,1)} %off_hbm.1), custom_call_target="tpu_custom_call" | custom-call | tf_op jit(solution)/shard_map/forward/pallas_call | solution.py:109
  3.8 0.5 %collective-permute-start = (bf16[4,8,16,128]{3,2,1,0:T(8,128)(2,1)S(1)}, bf16[4,8,16,128]{3,2,1,0:T(8,128)(2,1)S(1)}, u32[]{:S(2)}, u32[]{:S(2)}) collective-permute-start(bf16[4,8,16,128]{3,2,1,0:T(8,128)(2,1)S(1)} %get-tuple-element.11), channel_id=1, source_target_pairs={{0,1},{1,0},{2,3},{3,2},{4,5},{5,4},{6,7},{7,6},{8,9},{9,8},{10,11... | collective-permute-start | bytes 393224 | tf_op jit(solution)/shard_map/ppermute | solution.py:278
  4.3 0.0 copy-done.4
  4.3 0.0 copy-done.3
  4.3 0.0 copy-done.2
  4.3 0.1 prepare.1
  4.4 0.9 %collective-permute-done.refs_1_ = bf16[4,8,16,128]{3,2,1,0:T(8,128)(2,1)S(1)} collective-permute-done((bf16[4,8,16,128]{3,2,1,0:T(8,128)(2,1)S(1)}, bf16[4,8,16,128]{3,2,1,0:T(8,128)(2,1)S(1)}, u32[]{:S(2)}, u32[]{:S(2)}) %collective-permute-start) | collective-permute-done | bytes 131104 | tf_op jit(solution)/shard_map/ppermute | solution.py:278
  5.3 15.2 %all_to_all.10.parts = bf16[32,1,16,128]{3,2,1,0:T(8,128)(2,1)S(1)} all-to-all(bf16[32,1,16,128]{3,2,1,0:T(8,128)(2,1)S(1)} %bitcast.5), channel_id=1, replica_groups=mesh['row'=4,'z'=4,'core'=2] {'row','z','core'}, dimensions={0} | all-to-all | bytes 262144 | tf_op jit(solution)/shard_map/all_to_all | solution.py:302
  20.5 0.0 copy-start
  20.5 0.0 copy-start.1
  20.5 0.2 parent_solve.1
  20.6 10.0 %all_to_all.11 = bf16[32,1,16,128]{3,2,1,0:T(8,128)(2,1)S(1)} all-to-all(bf16[32,1,16,128]{3,2,1,0:T(8,128)(2,1)S(1)} %parent_solve.1), channel_id=1, replica_groups=mesh['row'=4,'z'=4,'core'=2] {'row','z','core'}, dimensions={0} | all-to-all | bytes 262144 | tf_op jit(solution)/shard_map/all_to_all | solution.py:304
  30.7 0.0 copy-start.5
  30.7 0.3 collective-permute-start.1
  31.0 0.0 copy-done
  31.0 0.0 copy-done.1
  31.0 0.6 %couple.1.coupled = bf16[48,128,128]{2,1,0:T(8,128)(2,1)S(1)} custom-call(bf16[48,128,128]{2,1,0:T(8,128)(2,1)S(1)} %copy-done, bf16[48,128,128]{2,1,0:T(8,128)(2,1)S(1)} %copy-done.1, bf16[4,8,16,128]{3,2,1,0:T(8,128)(2,1)S(1)} %bitcast.3), custom_call_target="tpu_custom_call" | custom-call | flops 201326592 | bytes 4718592 | tf_op jit(solution)/shard_map/couple/pallas_call | solution.py:136
  31.5 0.5 %collective-permute-done.1.rest_1_ = bf16[4,8,16,128]{3,2,1,0:T(8,128)(2,1)S(1)} collective-permute-done((bf16[4,8,16,128]{3,2,1,0:T(8,128)(2,1)S(1)}, bf16[4,8,16,128]{3,2,1,0:T(8,128)(2,1)S(1)}, u32[]{:S(2)}, u32[]{:S(2)}) %collective-permute-start.1) | collective-permute-done | bytes 131104 | tf_op jit(solution)/shard_map/ppermute | solution.py:278
  32.0 0.0 copy-done.5
  32.0 1.9 %backward.1 = (bf16[48,128,128]{2,1,0:T(8,128)(2,1)}, bf16[1,128,128]{2,1,0:T(8,128)(2,1)}) custom-call(s32[48]{0:T(128)S(1)} %copy-done.5, bf16[48,128,128]{2,1,0:T(8,128)(2,1)S(1)} %get-tuple-element.7.fwd, bf16[48,128,128]{2,1,0:T(8,128)(2,1)S(1)} %copy-done, bf16[48,128,128]{2,1,0:T(8,128)(2,1)S(1)} %couple.1.coupled, ...), custom_call_target="tpu_custom_call" | custom-call | tf_op jit(solution)/shard_map/backward/pallas_call | solution.py:257
  (1 shorter events, 0.0 us)
Async XLA Ops:
  0.6 3.6 %copy-start.4 = (bf16[1,128,128]{2,1,0:T(8,128)(2,1)S(1)}, bf16[1,128,128]{2,1,0:T(8,128)(2,1)}, u32[]{:S(2)}) copy-start(bf16[1,128,128]{2,1,0:T(8,128)(2,1)} %upper.1) | copy-start | bytes 98308
  0.6 3.6 %copy-start.3 = (bf16[1,128,128]{2,1,0:T(8,128)(2,1)S(1)}, bf16[1,128,128]{2,1,0:T(8,128)(2,1)}, u32[]{:S(2)}) copy-start(bf16[1,128,128]{2,1,0:T(8,128)(2,1)} %lower.1) | copy-start | bytes 98308
  0.7 3.6 %copy-start.2 = (bf16[1,128,128]{2,1,0:T(8,128)(2,1)S(1)}, bf16[1,128,128]{2,1,0:T(8,128)(2,1)}, u32[]{:S(2)}) copy-start(bf16[1,128,128]{2,1,0:T(8,128)(2,1)} %rhs.1) | copy-start | bytes 98308
  3.8 1.5 %collective-permute-start = (bf16[4,8,16,128]{3,2,1,0:T(8,128)(2,1)S(1)}, bf16[4,8,16,128]{3,2,1,0:T(8,128)(2,1)S(1)}, u32[]{:S(2)}, u32[]{:S(2)}) collective-permute-start(bf16[4,8,16,128]{3,2,1,0:T(8,128)(2,1)S(1)} %get-tuple-element.11), channel_id=1, source_target_pairs={{0,1},{1,0},{2,3},{3,2},{4,5},{5,4},{6,7},{7,6},{8,9},{9,8},{10,11... | collective-permute-start | bytes 393224 | tf_op jit(solution)/shard_map/ppermute | solution.py:278
  20.5 10.5 %copy-start = (bf16[48,128,128]{2,1,0:T(8,128)(2,1)S(1)}, bf16[48,128,128]{2,1,0:T(8,128)(2,1)}, u32[]{:S(2)}) copy-start(bf16[48,128,128]{2,1,0:T(8,128)(2,1)} %inv.3) | copy-start | bytes 4718596
  20.5 10.5 %copy-start.1 = (bf16[48,128,128]{2,1,0:T(8,128)(2,1)S(1)}, bf16[48,128,128]{2,1,0:T(8,128)(2,1)}, u32[]{:S(2)}) copy-start(bf16[48,128,128]{2,1,0:T(8,128)(2,1)} %off.1) | copy-start | bytes 4718596
  30.7 1.4 %copy-start.5 = (s32[48]{0:T(128)S(1)}, s32[48]{0:T(128)}, u32[]{:S(2)}) copy-start(s32[48]{0:T(128)} %owner.1) | copy-start | bytes 580
  30.7 1.3 %collective-permute-start.1 = (bf16[4,8,16,128]{3,2,1,0:T(8,128)(2,1)S(1)}, bf16[4,8,16,128]{3,2,1,0:T(8,128)(2,1)S(1)}, u32[]{:S(2)}, u32[]{:S(2)}) collective-permute-start(bf16[4,8,16,128]{3,2,1,0:T(8,128)(2,1)S(1)} %bitcast.2), channel_id=1, source_target_pairs={{0,1},{1,0},{2,3},{3,2},{4,5},{5,4},{6,7},{7,6},{8,9},{9,8},{10,11... | collective-permute-start | bytes 393224 | tf_op jit(solution)/shard_map/ppermute | solution.py:278
where the time goes:
time: 34 us; the launch traced here: 33.9 us
  blocking collectives  25.2 us (74%)
  Pallas kernels  5.83 us (17%)
  waiting for transfers between devices  1.31 us (4%)
  starting transfers between devices  0.83 us (2%)
  between operations  0.69 us (2%)
    all_to_all x1, blocking collectives, on_device(): parts = lax.all_to_all(sent, axes, 0, 0, tiled=True)  15.2 us
    all_to_all x1, blocking collectives, on_device(): mine = lax.all_to_all(solved, axes, 0, 0, tiled=True).reshape(total.shape)  10 us
    pallas_call x1, Pallas kernels, forward(): pl.pallas_call(functools.partial(forward_kernel, cores, chunk), out_shape...  3.09 us
    pallas_call x1, Pallas kernels, backward(): pl.pallas_call(functools.partial(backward_kernel, len(parts), groups), ou...  1.86 us
    ppermute x2, waiting for transfers between devices, from_core(): lax.ppermute(value, 'core', [(i, (i + k) % cores) for i in range(cores)])  1.31 us
    ppermute x2, starting transfers between devices, from_core(): lax.ppermute(value, 'core', [(i, (i + k) % cores) for i in range(cores)])  0.83 us
  transfers between devices with their start and end apart: 2, of which 2 were waited for; matrix products, arithmetic and copies ran while one was open for 0% of the time, Pallas kernels for 2%

commit v1 on v0

--- a/solution.py
+++ b/solution.py
@@ -101,7 +101,7 @@
 
 def forward(parent_of, rhs, inv, off, n_row, n_chip, cores, per_col):
     count, width, sides = rhs.shape
-    chunk = max(c for c in range(1, 13) if count % c == 0)
+    chunk = max(c for c in range(1, 17) if count % c == 0)
     parents = n_chip * cores * per_col
     piece = (n_row, parents, sides // (n_row * cores), width)
     kept = 2 * rhs.size + 2 * cores * math.prod(piece)

time: 34 us -> 34.1 us (level)
  no operation moved by 1% of the time
where the time goes in v1:
time: 34.1 us; the launch traced here: 33.9 us
  blocking collectives  25.2 us (74%)
  Pallas kernels  5.85 us (17%)
  waiting for transfers between devices  1.31 us (4%)
  starting transfers between devices  0.83 us (2%)
  between operations  0.69 us (2%)
    all_to_all x1, blocking collectives, on_device(): parts = lax.all_to_all(sent, axes, 0, 0, tiled=True)  15.2 us
    all_to_all x1, blocking collectives, on_device(): mine = lax.all_to_all(solved, axes, 0, 0, tiled=True).reshape(total.shape)  10 us
    pallas_call x1, Pallas kernels, forward(): pl.pallas_call(functools.partial(forward_kernel, cores, chunk), out_shape...  3.11 us
    pallas_call x1, Pallas kernels, backward(): pl.pallas_call(functools.partial(backward_kernel, len(parts), groups), ou...  1.86 us
    ppermute x2, waiting for transfers between devices, from_core(): lax.ppermute(value, 'core', [(i, (i + k) % cores) for i in range(cores)])  1.31 us
    ppermute x2, starting transfers between devices, from_core(): lax.ppermute(value, 'core', [(i, (i + k) % cores) for i in range(cores)])  0.83 us
  transfers between devices with their start and end apart: 2, of which 2 were waited for; matrix products, arithmetic and copies ran while one was open for 0% of the time, Pallas kernels for 2%

profile of v1, /device:TPU:0, one launch (start us, length us, event | category | flops | bytes accessed | tf_op | source)
XLA Modules:
  0.0 33.9 jit_solution(9566052763808495425)
XLA Ops:
  0.6 0.0 copy-start.4
  0.6 0.0 copy-start.3
  0.7 0.0 copy-start.2
  0.7 3.1 %forward.1 = (bf16[48,128,128]{2,1,0:T(8,128)(2,1)S(1)}, bf16[4,8,16,128]{3,2,1,0:T(8,128)(2,1)S(1)}, bf16[4,8,16,128]{3,2,1,0:T(8,128)(2,1)S(1)}) custom-call(s32[48]{0:T(128)} %owner.1, bf16[48,128,128]{2,1,0:T(8,128)(2,1)} %rhs_hbm.1, bf16[48,128,128]{2,1,0:T(8,128)(2,1)} %inv_hbm.1, bf16[48,128,128]{2,1,0:T(8,128)(2,1)} %off_hbm.1), custom_call_target="tpu_custom_call" | custom-call | tf_op jit(solution)/shard_map/forward/pallas_call | solution.py:109
  3.8 0.5 %collective-permute-start = (bf16[4,8,16,128]{3,2,1,0:T(8,128)(2,1)S(1)}, bf16[4,8,16,128]{3,2,1,0:T(8,128)(2,1)S(1)}, u32[]{:S(2)}, u32[]{:S(2)}) collective-permute-start(bf16[4,8,16,128]{3,2,1,0:T(8,128)(2,1)S(1)} %get-tuple-element.11), channel_id=1, source_target_pairs={{0,1},{1,0},{2,3},{3,2},{4,5},{5,4},{6,7},{7,6},{8,9},{9,8},{10,11... | collective-permute-start | bytes 393224 | tf_op jit(solution)/shard_map/ppermute | solution.py:278
  4.3 0.0 copy-done.4
  4.3 0.0 copy-done.3
  4.3 0.0 copy-done.2
  4.3 0.1 prepare.1
  4.4 0.9 %collective-permute-done.refs_1_ = bf16[4,8,16,128]{3,2,1,0:T(8,128)(2,1)S(1)} collective-permute-done((bf16[4,8,16,128]{3,2,1,0:T(8,128)(2,1)S(1)}, bf16[4,8,16,128]{3,2,1,0:T(8,128)(2,1)S(1)}, u32[]{:S(2)}, u32[]{:S(2)}) %collective-permute-start) | collective-permute-done | bytes 131104 | tf_op jit(solution)/shard_map/ppermute | solution.py:278
  5.3 15.2 %all_to_all.10.parts = bf16[32,1,16,128]{3,2,1,0:T(8,128)(2,1)S(1)} all-to-all(bf16[32,1,16,128]{3,2,1,0:T(8,128)(2,1)S(1)} %bitcast.5), channel_id=1, replica_groups=mesh['row'=4,'z'=4,'core'=2] {'row','z','core'}, dimensions={0} | all-to-all | bytes 262144 | tf_op jit(solution)/shard_map/all_to_all | solution.py:302
  20.5 0.0 copy-start
  20.5 0.0 copy-start.1
  20.5 0.2 parent_solve.1
  20.7 10.0 %all_to_all.11 = bf16[32,1,16,128]{3,2,1,0:T(8,128)(2,1)S(1)} all-to-all(bf16[32,1,16,128]{3,2,1,0:T(8,128)(2,1)S(1)} %parent_solve.1), channel_id=1, replica_groups=mesh['row'=4,'z'=4,'core'=2] {'row','z','core'}, dimensions={0} | all-to-all | bytes 262144 | tf_op jit(solution)/shard_map/all_to_all | solution.py:304
  30.7 0.0 copy-start.5
  30.7 0.3 collective-permute-start.1
  31.0 0.0 copy-done
  31.0 0.0 copy-done.1
  31.0 0.6 %couple.1.coupled = bf16[48,128,128]{2,1,0:T(8,128)(2,1)S(1)} custom-call(bf16[48,128,128]{2,1,0:T(8,128)(2,1)S(1)} %copy-done, bf16[48,128,128]{2,1,0:T(8,128)(2,1)S(1)} %copy-done.1, bf16[4,8,16,128]{3,2,1,0:T(8,128)(2,1)S(1)} %bitcast.3), custom_call_target="tpu_custom_call" | custom-call | flops 201326592 | bytes 4718592 | tf_op jit(solution)/shard_map/couple/pallas_call | solution.py:136
  31.6 0.5 %collective-permute-done.1.rest_1_ = bf16[4,8,16,128]{3,2,1,0:T(8,128)(2,1)S(1)} collective-permute-done((bf16[4,8,16,128]{3,2,1,0:T(8,128)(2,1)S(1)}, bf16[4,8,16,128]{3,2,1,0:T(8,128)(2,1)S(1)}, u32[]{:S(2)}, u32[]{:S(2)}) %collective-permute-start.1) | collective-permute-done | bytes 131104 | tf_op jit(solution)/shard_map/ppermute | solution.py:278
  32.0 0.0 copy-done.5
  32.0 1.9 %backward.1 = (bf16[48,128,128]{2,1,0:T(8,128)(2,1)}, bf16[1,128,128]{2,1,0:T(8,128)(2,1)}) custom-call(s32[48]{0:T(128)S(1)} %copy-done.5, bf16[48,128,128]{2,1,0:T(8,128)(2,1)S(1)} %get-tuple-element.7.fwd, bf16[48,128,128]{2,1,0:T(8,128)(2,1)S(1)} %copy-done, bf16[48,128,128]{2,1,0:T(8,128)(2,1)S(1)} %couple.1.coupled, ...), custom_call_target="tpu_custom_call" | custom-call | tf_op jit(solution)/shard_map/backward/pallas_call | solution.py:257
  (1 shorter events, 0.0 us)
Async XLA Ops:
  0.6 3.7 %copy-start.4 = (bf16[1,128,128]{2,1,0:T(8,128)(2,1)S(1)}, bf16[1,128,128]{2,1,0:T(8,128)(2,1)}, u32[]{:S(2)}) copy-start(bf16[1,128,128]{2,1,0:T(8,128)(2,1)} %upper.1) | copy-start | bytes 98308
  0.6 3.7 %copy-start.3 = (bf16[1,128,128]{2,1,0:T(8,128)(2,1)S(1)}, bf16[1,128,128]{2,1,0:T(8,128)(2,1)}, u32[]{:S(2)}) copy-start(bf16[1,128,128]{2,1,0:T(8,128)(2,1)} %lower.1) | copy-start | bytes 98308
  0.7 3.7 %copy-start.2 = (bf16[1,128,128]{2,1,0:T(8,128)(2,1)S(1)}, bf16[1,128,128]{2,1,0:T(8,128)(2,1)}, u32[]{:S(2)}) copy-start(bf16[1,128,128]{2,1,0:T(8,128)(2,1)} %rhs.1) | copy-start | bytes 98308
  3.8 1.5 %collective-permute-start = (bf16[4,8,16,128]{3,2,1,0:T(8,128)(2,1)S(1)}, bf16[4,8,16,128]{3,2,1,0:T(8,128)(2,1)S(1)}, u32[]{:S(2)}, u32[]{:S(2)}) collective-permute-start(bf16[4,8,16,128]{3,2,1,0:T(8,128)(2,1)S(1)} %get-tuple-element.11), channel_id=1, source_target_pairs={{0,1},{1,0},{2,3},{3,2},{4,5},{5,4},{6,7},{7,6},{8,9},{9,8},{10,11... | collective-permute-start | bytes 393224 | tf_op jit(solution)/shard_map/ppermute | solution.py:278
  20.5 10.5 %copy-start = (bf16[48,128,128]{2,1,0:T(8,128)(2,1)S(1)}, bf16[48,128,128]{2,1,0:T(8,128)(2,1)}, u32[]{:S(2)}) copy-start(bf16[48,128,128]{2,1,0:T(8,128)(2,1)} %inv.3) | copy-start | bytes 4718596
  20.5 10.5 %copy-start.1 = (bf16[48,128,128]{2,1,0:T(8,128)(2,1)S(1)}, bf16[48,128,128]{2,1,0:T(8,128)(2,1)}, u32[]{:S(2)}) copy-start(bf16[48,128,128]{2,1,0:T(8,128)(2,1)} %off.1) | copy-start | bytes 4718596
  30.7 1.4 %copy-start.5 = (s32[48]{0:T(128)S(1)}, s32[48]{0:T(128)}, u32[]{:S(2)}) copy-start(s32[48]{0:T(128)} %owner.1) | copy-start | bytes 580
  30.7 1.3 %collective-permute-start.1 = (bf16[4,8,16,128]{3,2,1,0:T(8,128)(2,1)S(1)}, bf16[4,8,16,128]{3,2,1,0:T(8,128)(2,1)S(1)}, u32[]{:S(2)}, u32[]{:S(2)}) collective-permute-start(bf16[4,8,16,128]{3,2,1,0:T(8,128)(2,1)S(1)} %bitcast.2), channel_id=1, source_target_pairs={{0,1},{1,0},{2,3},{3,2},{4,5},{5,4},{6,7},{7,6},{8,9},{9,8},{10,11... | collective-permute-start | bytes 393224 | tf_op jit(solution)/shard_map/ppermute | solution.py:278

commit v2 on v0

--- a/solution.py
+++ b/solution.py
@@ -81,9 +81,9 @@
             add((g - 1) * chunk + n, odd if n % 2 else even)
 
     pl.loop(1, groups - 1)(step)
+    load(2, groups - 1).wait()
     if groups > 1:
         step(groups - 1)
-    load(2, groups - 1).wait()
     for n in range(chunk):
         add((groups - 1) * chunk + n, odd if n % 2 else even)
     me = lax.axis_index("core")

time: 34 us -> 34 us (level)
  no operation moved by 1% of the time
where the time goes in v2:
time: 34 us; the launch traced here: 33.9 us
  blocking collectives  25.2 us (74%)
  Pallas kernels  5.83 us (17%)
  waiting for transfers between devices  1.31 us (4%)
  starting transfers between devices  0.83 us (2%)
  between operations  0.69 us (2%)
    all_to_all x1, blocking collectives, on_device(): parts = lax.all_to_all(sent, axes, 0, 0, tiled=True)  15.2 us
    all_to_all x1, blocking collectives, on_device(): mine = lax.all_to_all(solved, axes, 0, 0, tiled=True).reshape(total.shape)  10 us
    pallas_call x1, Pallas kernels, forward(): pl.pallas_call(functools.partial(forward_kernel, cores, chunk), out_shape...  3.09 us
    pallas_call x1, Pallas kernels, backward(): pl.pallas_call(functools.partial(backward_kernel, len(parts), groups), ou...  1.86 us
    ppermute x2, waiting for transfers between devices, from_core(): lax.ppermute(value, 'core', [(i, (i + k) % cores) for i in range(cores)])  1.31 us
    ppermute x2, starting transfers between devices, from_core(): lax.ppermute(value, 'core', [(i, (i + k) % cores) for i in range(cores)])  0.83 us
  transfers between devices with their start and end apart: 2, of which 2 were waited for; matrix products, arithmetic and copies ran while one was open for 0% of the time, Pallas kernels for 2%

profile of v2, /device:TPU:0, one launch (start us, length us, event | category | flops | bytes accessed | tf_op | source)
XLA Modules:
  0.0 33.9 jit_solution(14535471820727906595)
XLA Ops:
  0.6 0.0 copy-start.4
  0.6 0.0 copy-start.3
  0.7 0.0 copy-start.2
  0.7 3.1 %forward.1 = (bf16[48,128,128]{2,1,0:T(8,128)(2,1)S(1)}, bf16[4,8,16,128]{3,2,1,0:T(8,128)(2,1)S(1)}, bf16[4,8,16,128]{3,2,1,0:T(8,128)(2,1)S(1)}) custom-call(s32[48]{0:T(128)} %owner.1, bf16[48,128,128]{2,1,0:T(8,128)(2,1)} %rhs_hbm.1, bf16[48,128,128]{2,1,0:T(8,128)(2,1)} %inv_hbm.1, bf16[48,128,128]{2,1,0:T(8,128)(2,1)} %off_hbm.1), custom_call_target="tpu_custom_call" | custom-call | tf_op jit(solution)/shard_map/forward/pallas_call | solution.py:109
  3.8 0.5 %collective-permute-start = (bf16[4,8,16,128]{3,2,1,0:T(8,128)(2,1)S(1)}, bf16[4,8,16,128]{3,2,1,0:T(8,128)(2,1)S(1)}, u32[]{:S(2)}, u32[]{:S(2)}) collective-permute-start(bf16[4,8,16,128]{3,2,1,0:T(8,128)(2,1)S(1)} %get-tuple-element.11), channel_id=1, source_target_pairs={{0,1},{1,0},{2,3},{3,2},{4,5},{5,4},{6,7},{7,6},{8,9},{9,8},{10,11... | collective-permute-start | bytes 393224 | tf_op jit(solution)/shard_map/ppermute | solution.py:278
  4.3 0.0 copy-done.4
  4.3 0.0 copy-done.3
  4.3 0.0 copy-done.2
  4.3 0.1 prepare.1
  4.4 0.9 %collective-permute-done.refs_1_ = bf16[4,8,16,128]{3,2,1,0:T(8,128)(2,1)S(1)} collective-permute-done((bf16[4,8,16,128]{3,2,1,0:T(8,128)(2,1)S(1)}, bf16[4,8,16,128]{3,2,1,0:T(8,128)(2,1)S(1)}, u32[]{:S(2)}, u32[]{:S(2)}) %collective-permute-start) | collective-permute-done | bytes 131104 | tf_op jit(solution)/shard_map/ppermute | solution.py:278
  5.3 15.2 %all_to_all.10.parts = bf16[32,1,16,128]{3,2,1,0:T(8,128)(2,1)S(1)} all-to-all(bf16[32,1,16,128]{3,2,1,0:T(8,128)(2,1)S(1)} %bitcast.5), channel_id=1, replica_groups=mesh['row'=4,'z'=4,'core'=2] {'row','z','core'}, dimensions={0} | all-to-all | bytes 262144 | tf_op jit(solution)/shard_map/all_to_all | solution.py:302
  20.5 0.0 copy-start
  20.5 0.0 copy-start.1
  20.5 0.2 parent_solve.1
  20.6 10.0 %all_to_all.11 = bf16[32,1,16,128]{3,2,1,0:T(8,128)(2,1)S(1)} all-to-all(bf16[32,1,16,128]{3,2,1,0:T(8,128)(2,1)S(1)} %parent_solve.1), channel_id=1, replica_groups=mesh['row'=4,'z'=4,'core'=2] {'row','z','core'}, dimensions={0} | all-to-all | bytes 262144 | tf_op jit(solution)/shard_map/all_to_all | solution.py:304
  30.7 0.0 copy-start.5
  30.7 0.3 collective-permute-start.1
  31.0 0.0 copy-done
  31.0 0.0 copy-done.1
  31.0 0.6 %couple.1.coupled = bf16[48,128,128]{2,1,0:T(8,128)(2,1)S(1)} custom-call(bf16[48,128,128]{2,1,0:T(8,128)(2,1)S(1)} %copy-done, bf16[48,128,128]{2,1,0:T(8,128)(2,1)S(1)} %copy-done.1, bf16[4,8,16,128]{3,2,1,0:T(8,128)(2,1)S(1)} %bitcast.3), custom_call_target="tpu_custom_call" | custom-call | flops 201326592 | bytes 4718592 | tf_op jit(solution)/shard_map/couple/pallas_call | solution.py:136
  31.6 0.5 %collective-permute-done.1.rest_1_ = bf16[4,8,16,128]{3,2,1,0:T(8,128)(2,1)S(1)} collective-permute-done((bf16[4,8,16,128]{3,2,1,0:T(8,128)(2,1)S(1)}, bf16[4,8,16,128]{3,2,1,0:T(8,128)(2,1)S(1)}, u32[]{:S(2)}, u32[]{:S(2)}) %collective-permute-start.1) | collective-permute-done | bytes 131104 | tf_op jit(solution)/shard_map/ppermute | solution.py:278
  32.0 0.0 copy-done.5
  32.0 1.9 %backward.1 = (bf16[48,128,128]{2,1,0:T(8,128)(2,1)}, bf16[1,128,128]{2,1,0:T(8,128)(2,1)}) custom-call(s32[48]{0:T(128)S(1)} %copy-done.5, bf16[48,128,128]{2,1,0:T(8,128)(2,1)S(1)} %get-tuple-element.7.fwd, bf16[48,128,128]{2,1,0:T(8,128)(2,1)S(1)} %copy-done, bf16[48,128,128]{2,1,0:T(8,128)(2,1)S(1)} %couple.1.coupled, ...), custom_call_target="tpu_custom_call" | custom-call | tf_op jit(solution)/shard_map/backward/pallas_call | solution.py:257
  (1 shorter events, 0.0 us)
Async XLA Ops:
  0.6 3.6 %copy-start.4 = (bf16[1,128,128]{2,1,0:T(8,128)(2,1)S(1)}, bf16[1,128,128]{2,1,0:T(8,128)(2,1)}, u32[]{:S(2)}) copy-start(bf16[1,128,128]{2,1,0:T(8,128)(2,1)} %upper.1) | copy-start | bytes 98308
  0.6 3.6 %copy-start.3 = (bf16[1,128,128]{2,1,0:T(8,128)(2,1)S(1)}, bf16[1,128,128]{2,1,0:T(8,128)(2,1)}, u32[]{:S(2)}) copy-start(bf16[1,128,128]{2,1,0:T(8,128)(2,1)} %lower.1) | copy-start | bytes 98308
  0.7 3.6 %copy-start.2 = (bf16[1,128,128]{2,1,0:T(8,128)(2,1)S(1)}, bf16[1,128,128]{2,1,0:T(8,128)(2,1)}, u32[]{:S(2)}) copy-start(bf16[1,128,128]{2,1,0:T(8,128)(2,1)} %rhs.1) | copy-start | bytes 98308
  3.8 1.5 %collective-permute-start = (bf16[4,8,16,128]{3,2,1,0:T(8,128)(2,1)S(1)}, bf16[4,8,16,128]{3,2,1,0:T(8,128)(2,1)S(1)}, u32[]{:S(2)}, u32[]{:S(2)}) collective-permute-start(bf16[4,8,16,128]{3,2,1,0:T(8,128)(2,1)S(1)} %get-tuple-element.11), channel_id=1, source_target_pairs={{0,1},{1,0},{2,3},{3,2},{4,5},{5,4},{6,7},{7,6},{8,9},{9,8},{10,11... | collective-permute-start | bytes 393224 | tf_op jit(solution)/shard_map/ppermute | solution.py:278
  20.5 10.5 %copy-start = (bf16[48,128,128]{2,1,0:T(8,128)(2,1)S(1)}, bf16[48,128,128]{2,1,0:T(8,128)(2,1)}, u32[]{:S(2)}) copy-start(bf16[48,128,128]{2,1,0:T(8,128)(2,1)} %inv.3) | copy-start | bytes 4718596
  20.5 10.5 %copy-start.1 = (bf16[48,128,128]{2,1,0:T(8,128)(2,1)S(1)}, bf16[48,128,128]{2,1,0:T(8,128)(2,1)}, u32[]{:S(2)}) copy-start(bf16[48,128,128]{2,1,0:T(8,128)(2,1)} %off.1) | copy-start | bytes 4718596
  30.7 1.4 %copy-start.5 = (s32[48]{0:T(128)S(1)}, s32[48]{0:T(128)}, u32[]{:S(2)}) copy-start(s32[48]{0:T(128)} %owner.1) | copy-start | bytes 580
  30.7 1.3 %collective-permute-start.1 = (bf16[4,8,16,128]{3,2,1,0:T(8,128)(2,1)S(1)}, bf16[4,8,16,128]{3,2,1,0:T(8,128)(2,1)S(1)}, u32[]{:S(2)}, u32[]{:S(2)}) collective-permute-start(bf16[4,8,16,128]{3,2,1,0:T(8,128)(2,1)S(1)} %bitcast.2), channel_id=1, source_target_pairs={{0,1},{1,0},{2,3},{3,2},{4,5},{5,4},{6,7},{7,6},{8,9},{9,8},{10,11... | collective-permute-start | bytes 393224 | tf_op jit(solution)/shard_map/ppermute | solution.py:278

commit v3 on v0

--- a/solution.py
+++ b/solution.py
@@ -36,7 +36,7 @@
 
 def forward_kernel(cores, chunk, owner_hbm, rhs_hbm, inv_hbm, off_hbm, fwd, *rest):
     mine, theirs, scratch = rest[0], rest[1:cores], rest[cores:]
-    rhs, inv, off, owner, even, odd, in_sem, owner_sem = scratch
+    rhs, inv, off, owner, acc, in_sem, owner_sem = scratch
     n_row, _, half, _ = mine.shape
     groups = fwd.shape[0] // chunk
     arrays = ((rhs_hbm, rhs), (inv_hbm, inv), (off_hbm, off))
@@ -57,13 +57,12 @@
         load(2, g - 1).start()
 
     load(2, groups - 1).start()
-    even[...] = jnp.zeros_like(even)
-    odd[...] = jnp.zeros_like(odd)
+    acc[...] = jnp.zeros_like(acc)
 
     def solve(c):
         fwd[c] = dot(inv[c], rhs[c]).astype(BF16)
 
-    def add(c, acc):
+    def add(c):
         acc[owner[c]] += dot(off[c], fwd[c])
 
     load(0, 0).wait()
@@ -78,17 +77,17 @@
         load(2, g - 1).wait()
         for n in range(chunk):
             solve(g * chunk + n)
-            add((g - 1) * chunk + n, odd if n % 2 else even)
+            add((g - 1) * chunk + n)
 
     pl.loop(1, groups - 1)(step)
     if groups > 1:
         step(groups - 1)
     load(2, groups - 1).wait()
     for n in range(chunk):
-        add((groups - 1) * chunk + n, odd if n % 2 else even)
+        add((groups - 1) * chunk + n)
     me = lax.axis_index("core")
-    for p in range(even.shape[0]):
-        turned = (even[p] + odd[p]).astype(BF16).T
+    for p in range(acc.shape[0]):
+        turned = acc[p].astype(BF16).T
         for r in range(n_row):
             halves = [turned[n * half : (n + 1) * half] for n in range(r * cores, (r + 1) * cores)]
             for k in range(cores):
@@ -116,7 +115,6 @@
             pltpu.VMEM(inv.shape, BF16),
             pltpu.VMEM(off.shape, BF16),
             pltpu.SMEM(parent_of.shape, jnp.int32),
-            pltpu.VMEM((parents, width, sides), F32),
             pltpu.VMEM((parents, width, sides), F32),
             pltpu.SemaphoreType.DMA((3, count // chunk)),
             pltpu.SemaphoreType.DMA,

time: 34 us -> 34 us (level)
  no operation moved by 1% of the time
where the time goes in v3:
time: 34 us; the launch traced here: 33.9 us
  blocking collectives  25.2 us (74%)
  Pallas kernels  5.84 us (17%)
  waiting for transfers between devices  1.31 us (4%)
  starting transfers between devices  0.83 us (2%)
  between operations  0.69 us (2%)
    all_to_all x1, blocking collectives, on_device(): parts = lax.all_to_all(sent, axes, 0, 0, tiled=True)  15.2 us
    all_to_all x1, blocking collectives, on_device(): mine = lax.all_to_all(solved, axes, 0, 0, tiled=True).reshape(total.shape)  10 us
    pallas_call x1, Pallas kernels, forward(): pl.pallas_call(functools.partial(forward_kernel, cores, chunk), out_shape...  3.1 us
    pallas_call x1, Pallas kernels, backward(): pl.pallas_call(functools.partial(backward_kernel, len(parts), groups), ou...  1.86 us
    ppermute x2, waiting for transfers between devices, from_core(): lax.ppermute(value, 'core', [(i, (i + k) % cores) for i in range(cores)])  1.31 us
    ppermute x2, starting transfers between devices, from_core(): lax.ppermute(value, 'core', [(i, (i + k) % cores) for i in range(cores)])  0.83 us
  transfers between devices with their start and end apart: 2, of which 2 were waited for; matrix products, arithmetic and copies ran while one was open for 0% of the time, Pallas kernels for 2%

profile of v3, /device:TPU:0, one launch (start us, length us, event | category | flops | bytes accessed | tf_op | source)
XLA Modules:
  0.0 33.9 jit_solution(9437445778985706063)
XLA Ops:
  0.6 0.0 copy-start.4
  0.6 0.0 copy-start.3
  0.7 0.0 copy-start.2
  0.7 3.1 %forward.1 = (bf16[48,128,128]{2,1,0:T(8,128)(2,1)S(1)}, bf16[4,8,16,128]{3,2,1,0:T(8,128)(2,1)S(1)}, bf16[4,8,16,128]{3,2,1,0:T(8,128)(2,1)S(1)}) custom-call(s32[48]{0:T(128)} %owner.1, bf16[48,128,128]{2,1,0:T(8,128)(2,1)} %rhs_hbm.1, bf16[48,128,128]{2,1,0:T(8,128)(2,1)} %inv_hbm.1, bf16[48,128,128]{2,1,0:T(8,128)(2,1)} %off_hbm.1), custom_call_target="tpu_custom_call" | custom-call | tf_op jit(solution)/shard_map/forward/pallas_call | solution.py:108
  3.8 0.5 %collective-permute-start = (bf16[4,8,16,128]{3,2,1,0:T(8,128)(2,1)S(1)}, bf16[4,8,16,128]{3,2,1,0:T(8,128)(2,1)S(1)}, u32[]{:S(2)}, u32[]{:S(2)}) collective-permute-start(bf16[4,8,16,128]{3,2,1,0:T(8,128)(2,1)S(1)} %get-tuple-element.11), channel_id=1, source_target_pairs={{0,1},{1,0},{2,3},{3,2},{4,5},{5,4},{6,7},{7,6},{8,9},{9,8},{10,11... | collective-permute-start | bytes 393224 | tf_op jit(solution)/shard_map/ppermute | solution.py:276
  4.3 0.0 copy-done.4
  4.3 0.0 copy-done.3
  4.3 0.0 copy-done.2
  4.3 0.1 prepare.1
  4.4 0.9 %collective-permute-done.refs_1_ = bf16[4,8,16,128]{3,2,1,0:T(8,128)(2,1)S(1)} collective-permute-done((bf16[4,8,16,128]{3,2,1,0:T(8,128)(2,1)S(1)}, bf16[4,8,16,128]{3,2,1,0:T(8,128)(2,1)S(1)}, u32[]{:S(2)}, u32[]{:S(2)}) %collective-permute-start) | collective-permute-done | bytes 131104 | tf_op jit(solution)/shard_map/ppermute | solution.py:276
  5.3 15.2 %all_to_all.10.parts = bf16[32,1,16,128]{3,2,1,0:T(8,128)(2,1)S(1)} all-to-all(bf16[32,1,16,128]{3,2,1,0:T(8,128)(2,1)S(1)} %bitcast.5), channel_id=1, replica_groups=mesh['row'=4,'z'=4,'core'=2] {'row','z','core'}, dimensions={0} | all-to-all | bytes 262144 | tf_op jit(solution)/shard_map/all_to_all | solution.py:300
  20.5 0.0 copy-start
  20.5 0.0 copy-start.1
  20.5 0.2 parent_solve.1
  20.6 10.0 %all_to_all.11 = bf16[32,1,16,128]{3,2,1,0:T(8,128)(2,1)S(1)} all-to-all(bf16[32,1,16,128]{3,2,1,0:T(8,128)(2,1)S(1)} %parent_solve.1), channel_id=1, replica_groups=mesh['row'=4,'z'=4,'core'=2] {'row','z','core'}, dimensions={0} | all-to-all | bytes 262144 | tf_op jit(solution)/shard_map/all_to_all | solution.py:302
  30.7 0.0 copy-start.5
  30.7 0.3 collective-permute-start.1
  31.0 0.0 copy-done
  31.0 0.0 copy-done.1
  31.0 0.6 %couple.1.coupled = bf16[48,128,128]{2,1,0:T(8,128)(2,1)S(1)} custom-call(bf16[48,128,128]{2,1,0:T(8,128)(2,1)S(1)} %copy-done, bf16[48,128,128]{2,1,0:T(8,128)(2,1)S(1)} %copy-done.1, bf16[4,8,16,128]{3,2,1,0:T(8,128)(2,1)S(1)} %bitcast.3), custom_call_target="tpu_custom_call" | custom-call | flops 201326592 | bytes 4718592 | tf_op jit(solution)/shard_map/couple/pallas_call | solution.py:134
  31.6 0.5 %collective-permute-done.1.rest_1_ = bf16[4,8,16,128]{3,2,1,0:T(8,128)(2,1)S(1)} collective-permute-done((bf16[4,8,16,128]{3,2,1,0:T(8,128)(2,1)S(1)}, bf16[4,8,16,128]{3,2,1,0:T(8,128)(2,1)S(1)}, u32[]{:S(2)}, u32[]{:S(2)}) %collective-permute-start.1) | collective-permute-done | bytes 131104 | tf_op jit(solution)/shard_map/ppermute | solution.py:276
  32.0 0.0 copy-done.5
  32.0 1.9 %backward.1 = (bf16[48,128,128]{2,1,0:T(8,128)(2,1)}, bf16[1,128,128]{2,1,0:T(8,128)(2,1)}) custom-call(s32[48]{0:T(128)S(1)} %copy-done.5, bf16[48,128,128]{2,1,0:T(8,128)(2,1)S(1)} %get-tuple-element.7.fwd, bf16[48,128,128]{2,1,0:T(8,128)(2,1)S(1)} %copy-done, bf16[48,128,128]{2,1,0:T(8,128)(2,1)S(1)} %couple.1.coupled, ...), custom_call_target="tpu_custom_call" | custom-call | tf_op jit(solution)/shard_map/backward/pallas_call | solution.py:255
  (1 shorter events, 0.0 us)
Async XLA Ops:
  0.6 3.7 %copy-start.4 = (bf16[1,128,128]{2,1,0:T(8,128)(2,1)S(1)}, bf16[1,128,128]{2,1,0:T(8,128)(2,1)}, u32[]{:S(2)}) copy-start(bf16[1,128,128]{2,1,0:T(8,128)(2,1)} %upper.1) | copy-start | bytes 98308
  0.6 3.6 %copy-start.3 = (bf16[1,128,128]{2,1,0:T(8,128)(2,1)S(1)}, bf16[1,128,128]{2,1,0:T(8,128)(2,1)}, u32[]{:S(2)}) copy-start(bf16[1,128,128]{2,1,0:T(8,128)(2,1)} %lower.1) | copy-start | bytes 98308
  0.7 3.6 %copy-start.2 = (bf16[1,128,128]{2,1,0:T(8,128)(2,1)S(1)}, bf16[1,128,128]{2,1,0:T(8,128)(2,1)}, u32[]{:S(2)}) copy-start(bf16[1,128,128]{2,1,0:T(8,128)(2,1)} %rhs.1) | copy-start | bytes 98308
  3.8 1.5 %collective-permute-start = (bf16[4,8,16,128]{3,2,1,0:T(8,128)(2,1)S(1)}, bf16[4,8,16,128]{3,2,1,0:T(8,128)(2,1)S(1)}, u32[]{:S(2)}, u32[]{:S(2)}) collective-permute-start(bf16[4,8,16,128]{3,2,1,0:T(8,128)(2,1)S(1)} %get-tuple-element.11), channel_id=1, source_target_pairs={{0,1},{1,0},{2,3},{3,2},{4,5},{5,4},{6,7},{7,6},{8,9},{9,8},{10,11... | collective-permute-start | bytes 393224 | tf_op jit(solution)/shard_map/ppermute | solution.py:276
  20.5 10.5 %copy-start = (bf16[48,128,128]{2,1,0:T(8,128)(2,1)S(1)}, bf16[48,128,128]{2,1,0:T(8,128)(2,1)}, u32[]{:S(2)}) copy-start(bf16[48,128,128]{2,1,0:T(8,128)(2,1)} %inv.3) | copy-start | bytes 4718596
  20.5 10.5 %copy-start.1 = (bf16[48,128,128]{2,1,0:T(8,128)(2,1)S(1)}, bf16[48,128,128]{2,1,0:T(8,128)(2,1)}, u32[]{:S(2)}) copy-start(bf16[48,128,128]{2,1,0:T(8,128)(2,1)} %off.1) | copy-start | bytes 4718596
  30.7 1.4 %copy-start.5 = (s32[48]{0:T(128)S(1)}, s32[48]{0:T(128)}, u32[]{:S(2)}) copy-start(s32[48]{0:T(128)} %owner.1) | copy-start | bytes 580
  30.7 1.3 %collective-permute-start.1 = (bf16[4,8,16,128]{3,2,1,0:T(8,128)(2,1)S(1)}, bf16[4,8,16,128]{3,2,1,0:T(8,128)(2,1)S(1)}, u32[]{:S(2)}, u32[]{:S(2)}) collective-permute-start(bf16[4,8,16,128]{3,2,1,0:T(8,128)(2,1)S(1)} %bitcast.2), channel_id=1, source_target_pairs={{0,1},{1,0},{2,3},{3,2},{4,5},{5,4},{6,7},{7,6},{8,9},{9,8},{10,11... | collective-permute-start | bytes 393224 | tf_op jit(solution)/shard_map/ppermute | solution.py:276
